TPU v7x, 32 devices: a whole 2x2x4 slice. The times are simulated.
32 devices in a mesh: depth: 2 (over x), row: 4 (over z), col: 4 (over y, core).
Axes of the slice: x: 2, y: 2, z: 4, core: 2. Of those that a mesh axis runs over, the one named last changes fastest.
Arguments:
- inputs: bfloat16 [512, 6144], P('depth', 'row'), may hold values from -6 to 6
- weight: bfloat16 [6144, 24576], P('row', 'col'), may hold values from -0.078125 to 0.078125
- cotangent: bfloat16 [512, 4, 6144], P('depth', 'col', 'row'), may hold values from -6 to 6
Outputs:
- activated: bfloat16 [512, 4, 6144], P('depth', 'col', 'row')
- input_grad: bfloat16 [512, 6144], P('depth', 'row')
- weight_grad: bfloat16 [6144, 4, 6144], P('row', 'col', 'depth')
All inputs are finite; a program needn't handle non-finite values.
Results may differ from a plain program's by a relative error of at most 0.005.
Values may be sent and summed in bfloat16 or wider, within the bound.
A program may use at most 128 MiB of HBM per device.

v0:
```python
import jax
import jax.numpy as jnp
from jax import lax
from jax.sharding import PartitionSpec as P

root_two_pi = 0.7978845608028654
cubic = 0.044715


def activate(hidden):
    inner = root_two_pi * (hidden + cubic * hidden * hidden * hidden)
    return (0.5 * hidden * (1.0 + jnp.tanh(inner))).astype(jnp.bfloat16)


def gelu_slope(hidden):
    tanh_val = jnp.tanh(root_two_pi * (hidden + cubic * hidden * hidden * hidden))
    return 0.5 * (1.0 + tanh_val) + 0.5 * hidden * (1.0 - tanh_val * tanh_val) * root_two_pi * (
        1.0 + 3.0 * cubic * hidden * hidden
    )


def local(inputs, weight, cotangent):
    hidden_own = lax.psum_scatter(
        lax.dot_general(
            weight, inputs, (((0,), (1,)), ((), ())), preferred_element_type=jnp.float32
        ),
        "row",
        scatter_dimension=0,
        tiled=True,
    ).T
    activated = activate(hidden_own)[:, None, :]
    grad_own = (cotangent[:, 0, :].astype(jnp.float32) * gelu_slope(hidden_own)).astype(
        jnp.bfloat16
    )
    grad_hidden = lax.all_gather(grad_own, "row", axis=1, tiled=True)
    input_term = lax.dot_general(
        grad_hidden, weight, (((1,), (1,)), ((), ())), preferred_element_type=jnp.float32
    )
    input_grad = lax.psum(input_term, "col").astype(jnp.bfloat16)
    weight_term = lax.dot_general(
        inputs, grad_hidden, (((0,), (0,)), ((), ())), preferred_element_type=jnp.float32
    )
    weight_grad = lax.psum_scatter(
        weight_term[:, None, :], "depth", scatter_dimension=2, tiled=True
    ).astype(jnp.bfloat16)
    return (activated, input_grad, weight_grad)


def solution(mesh):
    placed = (P("depth", "row"), P("row", "col"), P("depth", "col", "row"))
    return jax.shard_map(
        local,
        mesh=mesh,
        in_specs=placed,
        out_specs=(P("depth", "col", "row"), P("depth", "row"), P("row", "col", "depth")),
        check_vma=False,
    )
```

profile of v0, /device:TPU:0, one launch (start us, length us, event | category | flops | bytes accessed | tf_op | source)
XLA Modules:
  0.0 661.3 jit_solution(2269290046150853597)
XLA Ops:
  7.2 0.0 copy-start
  7.2 0.0 reduce-scatter.3.cloned.1.call-start
  7.2 1.1 copy-done
  8.3 11.8 %fusion.8 = f32[6144,256]{1,0:T(8,128)} fusion(bf16[1536,6144]{1,0:T(8,128)(2,1)} %param.4, bf16[256,1536]{1,0:T(8,128)(2,1)S(1)} %copy-done), kind=kOutput, calls=%fused_computation.13 | convolution fusion | flops 4831838208 | bytes 25952256 | tf_op jit(solution)/shard_map/dot_general | solution.py:24
  20.1 0.0 copy-start.2
  20.1 0.0 reduce-scatter.3.cloned.1.call-update
  20.2 0.0 all-gather.2.cloned.1.call-start
  20.2 1.1 copy-done.2
  21.3 0.3 copy.6
  21.5 112.2 %reduce-scatter.3.cloned.1.call-done = f32[1536,256]{1,0:T(8,128)} async-done(((f32[6144,256]{1,0:T(8,128)}), f32[1536,256]{1,0:T(8,128)}) %reduce-scatter.3.cloned.1.call-update) | async-done | bytes 1572880 | tf_op jit(solution)/shard_map/reduce_scatter | solution.py:23
  133.8 3.4 fusion.6
  137.2 0.0 all-gather.2.cloned.1.call-update
  137.2 0.0 reduce-scatter.5.cloned.1.call-start
  137.3 64.1 %all-gather.2.cloned.1.call-done = bf16[256,6144]{0,1:T(8,128)(2,1)} async-done(((bf16[256,1536]{0,1:T(8,128)(2,1)}), bf16[256,6144]{0,1:T(8,128)(2,1)}) %all-gather.2.cloned.1.call-update) | async-done | bytes 3145744 | tf_op jit(solution)/shard_map/all_gather | solution.py:35
  201.4 16.7 %convolution_bitcast_fusion = f32[1536,1,6144]{0,2,1:T(8,128)} fusion(bf16[256,6144]{0,1:T(8,128)(2,1)} %all-gather.2.cloned.1.call-done, bf16[256,1536]{1,0:T(8,128)(2,1)S(1)} %copy-done), kind=kOutput, calls=%fused_computation | convolution fusion | flops 4831838208 | bytes 41680896 | tf_op jit(solution)/shard_map/dot_general | solution.py:40
  218.1 0.0 reduce-scatter.5.cloned.1.call-update
  218.1 1.2 copy.7
  219.3 10.7 %fusion.9 = f32[256,1536]{1,0:T(8,128)S(1)} fusion(bf16[256,6144]{0,1:T(8,128)(2,1)} %all-gather.2.cloned.1.call-done, bf16[1536,6144]{1,0:T(8,128)(2,1)} %param.4), kind=kOutput, calls=%fused_computation.14 | convolution fusion | flops 4831838208 | bytes 23592960 | tf_op jit(solution)/shard_map/dot_general | solution.py:36
  230.0 33.4 %all-reduce.1 = bf16[256,1536]{1,0:T(8,128)(2,1)} all-reduce(f32[256,1536]{1,0:T(8,128)S(1)} %fusion.9), channel_id=1, replica_groups=mesh['depth'=2,'row'=4,'col'=4] {'col'}, use_global_device_ids=true, to_apply=%region_1.0 | all-reduce | flops 393216 | bytes 2359296 | tf_op jit(solution)/shard_map/psum | solution.py:39
  263.4 367.4 %reduce-scatter.5.cloned.1.call-done = f32[1536,1,3072]{0,2,1:T(8,128)} async-done(((f32[1536,1,6144]{0,2,1:T(8,128)}), f32[1536,1,3072]{0,2,1:T(8,128)}) %reduce-scatter.5.cloned.1.call-update) | async-done | bytes 18874384 | tf_op jit(solution)/shard_map/reduce_scatter | solution.py:43
  630.8 11.3 %convert_element_type.23 = bf16[1536,1,3072]{0,2,1:T(8,128)(2,1)} convert(f32[1536,1,3072]{0,2,1:T(8,128)} %reduce-scatter.5.cloned.1.call-done) | non-fusion elementwise | flops 4718592 | bytes 28311552 | tf_op jit(solution)/shard_map/convert_element_type | solution.py:45
  642.1 0.0 copy-start.1
  642.1 12.7 %copy.8 = bf16[1536,1,3072]{2,0,1:T(8,128)(2,1)} copy(bf16[1536,1,3072]{0,2,1:T(8,128)(2,1)} %convert_element_type.23) | data formatting | bytes 18874368
  654.8 0.0 copy-done.1
Async XLA Ops:
  7.2 1.1 copy-start
  7.2 126.6 %reduce-scatter.3.cloned.1.call-start = ((), (), s32[]{:S(2)}) async-start(), calls=%async_computation.2 | async-start | bytes 7864320 | tf_op jit(solution)/shard_map/reduce_scatter | solution.py:23
  20.1 1.1 copy-start.2
  20.2 181.2 %all-gather.2.cloned.1.call-start = ((), (), s32[]{:S(2)}) async-start(), calls=%async_computation.3 | async-start | bytes 3932160 | tf_op jit(solution)/shard_map/all_gather | solution.py:35
  137.2 493.6 %reduce-scatter.5.cloned.1.call-start = ((), (), s32[]{:S(2)}) async-start(), calls=%async_computation.4 | async-start | bytes 56623104 | tf_op jit(solution)/shard_map/reduce_scatter | solution.py:43
  642.1 12.7 %copy-start.1 = (bf16[256,1536]{1,0:T(8,128)(2,1)S(1)}, bf16[256,1536]{1,0:T(8,128)(2,1)}, u32[]{:S(2)}) copy-start(bf16[256,1536]{1,0:T(8,128)(2,1)} %param.3) | copy-start | bytes 2359300
Sparse Core Ops, SparseCore 0:
  20.3 113.4 reduce-scatter.2
  137.3 64.0 all-gather.1
  218.2 412.5 reduce-scatter.4
where the time goes:
time: 662 us; the launch traced here: 661 us
  waiting for transfers between devices  544 us (82%)
  matrix products  39.2 us (6%)
  blocking collectives  33.4 us (5%)
  local copies, waits for them, and re-layouts  16.2 us (2%)
  other arithmetic  14.7 us (2%)
  between operations  13.8 us (2%)
    reduce_scatter x1, waiting for transfers between devices, local(): lax.psum_scatter(weight_term[:, None, :], 'depth', scatter_dimension=2, t...  367 us
    reduce_scatter x1, waiting for transfers between devices, local(): lax.psum_scatter(lax.dot_general(weight, inputs, (((0,), (1,)), ((), ()))...  112 us
    all_gather x1, waiting for transfers between devices, local(): grad_hidden = lax.all_gather(grad_own, 'row', axis=1, tiled=True)  64.1 us
    psum x1, blocking collectives, local(): input_grad = lax.psum(input_term, 'col').astype(jnp.bfloat16)  33.4 us
    dot_general x1, matrix products, local(): lax.dot_general(inputs, grad_hidden, (((0,), (0,)), ((), ())), preferred_...  16.7 us
    unnamed x9, local copies, waits for them, and re-layouts  16.2 us
  transfers between devices with their start and end apart: 3, of which 3 were waited for; matrix products, arithmetic and copies ran while one was open for 2% of the time, Pallas kernels for 0%

commit v1 on v0

v1 whole, which is shorter than its diff:
```python
import functools

import jax
import jax.numpy as jnp
from jax import lax
from jax.experimental import pallas as pl
from jax.experimental.pallas import tpu as pltpu
from jax.sharding import PartitionSpec as P

root_two_pi = 0.7978845608028654
cubic = 0.044715
MESH = pl.DeviceIdType.MESH


def remote(src, dst, send_sem, recv_sem, where):
    return pltpu.make_async_remote_copy(
        src_ref=src,
        dst_ref=dst,
        send_sem=send_sem,
        recv_sem=recv_sem,
        device_id=where,
        device_id_type=MESH,
    )


def kernel(
    rows, depths, cols, x_ref, w_hbm, cot_hbm,
    act_out, grad_out, x_all, g_all,
    w_buf, part, s_buf, r_buf, l_buf, g_buf, cot_buf, act_buf, acc, out_buf, in_buf,
    w_sem, cot_sem, act_sem, s_sem, r_sem, l_sem, g_sem, gr_sem, gl_sem, xs_sem, xr_sem,
    in_sem, out_sem, cs_sem, cr_sem,
):
    r, d, c = lax.axis_index("row"), lax.axis_index("depth"), lax.axis_index("col")
    tokens, features = x_ref.shape
    chunk = w_buf.shape[2]
    steps = w_buf.shape[0] // rows
    width = steps * chunk
    per = rows // depths
    last = rows - 1
    twin = c + 1 - 2 * lax.rem(c, 2)
    bits = cols.bit_length() - 1

    def flip(bit):
        size = 1 << bit
        return c + size - 2 * size * lax.rem(c // size, 2)

    def w_copy(q, k):
        j = q * steps + k
        at = pl.multiple_of(q * width + k * chunk, chunk)
        return pltpu.make_async_copy(w_hbm.at[:, pl.ds(at, chunk)], w_buf.at[j], w_sem.at[j])

    def cot_copy(k):
        at = pl.multiple_of(k * chunk, chunk)
        return pltpu.make_async_copy(cot_hbm.at[:, pl.ds(at, chunk)], cot_buf.at[k], cot_sem.at[k])

    def act_copy(k):
        at = pl.multiple_of(k * chunk, chunk)
        return pltpu.make_async_copy(act_buf.at[k], act_out.at[:, pl.ds(at, chunk)], act_sem.at[k])

    def right(j):
        return remote(s_buf.at[j], r_buf.at[j], s_sem.at[j], r_sem.at[j], {"row": r + 1})

    def left(j):
        return remote(s_buf.at[j], l_buf.at[j], s_sem.at[j], l_sem.at[j], {"row": r - 1})

    def g_right(j):
        return remote(g_buf.at[j], g_buf.at[j], gr_sem.at[j], g_sem.at[j], {"row": r + 1})

    def g_left(j):
        return remote(g_buf.at[j], g_buf.at[j], gl_sem.at[j], g_sem.at[j], {"row": r - 1})

    def g_place(source, q, k):
        at = pl.multiple_of(lax.rem(q, per) * width + k * chunk, chunk)
        return g_all.at[pl.ds(pl.multiple_of(source * tokens, tokens), tokens), pl.ds(at, chunk)]

    def g_over(q, k):
        j = q * steps + k
        slot = (d * per + lax.rem(q, per)) * steps + k
        return remote(
            g_buf.at[j], g_place(d, q, k), xs_sem.at[j], xr_sem.at[slot], {"depth": q // per}
        )

    def g_keep(q, k):
        j = q * steps + k
        return pltpu.make_async_copy(g_buf.at[j], g_place(d, q, k), xs_sem.at[j])

    def share(q, k):
        @pl.when(q // per != d)
        def _():
            g_over(q, k).start()

        @pl.when(q // per == d)
        def _():
            g_keep(q, k).start()

    def x_place(source):
        return x_all.at[pl.ds(pl.multiple_of(source * tokens, tokens), tokens), :]

    def x_over(target):
        return remote(
            x_ref, x_place(d), in_sem.at[target], out_sem.at[d], {"depth": target}
        )

    x_keep = pltpu.make_async_copy(x_ref, x_place(d), in_sem.at[d])

    for k in range(steps):
        for q in range(rows):
            w_copy(q, k).start()
        cot_copy(k).start()
    x_keep.start()

    barrier = pltpu.get_barrier_semaphore()

    @pl.when(r > 0)
    def _():
        pl.semaphore_signal(barrier, inc=1, device_id={"row": r - 1}, device_id_type=MESH)

    @pl.when(r < last)
    def _():
        pl.semaphore_signal(barrier, inc=1, device_id={"row": r + 1}, device_id_type=MESH)

    for off in range(1, depths):
        pl.semaphore_signal(
            barrier, inc=1, device_id={"depth": lax.rem(d + off, depths)}, device_id_type=MESH
        )
    for bit in range(bits):
        pl.semaphore_signal(barrier, inc=1, device_id={"col": flip(bit)}, device_id_type=MESH)

    @pl.when((r > 0) & (r < last))
    def _():
        pl.semaphore_wait(barrier, depths + bits + 1)

    @pl.when((r == 0) | (r == last))
    def _():
        pl.semaphore_wait(barrier, depths + bits)

    for off in range(1, depths):
        x_over(lax.rem(d + off, depths)).start()

    acc[...] = jnp.zeros_like(acc)

    def body(s, carry):
        @pl.when(s < steps)
        def _():
            for q in range(rows):
                j = q * steps + s
                w_copy(q, s).wait()
                part[j] = jnp.dot(x_ref[...], w_buf[j], preferred_element_type=jnp.float32)

        kr = s - r

        @pl.when((kr >= 0) & (kr < steps))
        def _():
            for q in range(last, 0, -1):
                @pl.when(q > r)
                def _():
                    j = q * steps + kr

                    @pl.when(r > 0)
                    def _():
                        right(j).wait_recv()
                        s_buf[j] = (part[j] + r_buf[j].astype(jnp.float32)).astype(jnp.bfloat16)

                    @pl.when(r == 0)
                    def _():
                        s_buf[j] = part[j].astype(jnp.bfloat16)

                    right(j).start()

        kl = s - (last - r)

        @pl.when((kl >= 0) & (kl < steps))
        def _():
            for q in range(last):
                @pl.when(q < r)
                def _():
                    j = q * steps + kl

                    @pl.when(r < last)
                    def _():
                        left(j).wait_recv()
                        s_buf[j] = (part[j] + l_buf[j].astype(jnp.float32)).astype(jnp.bfloat16)

                    @pl.when(r == last)
                    def _():
                        s_buf[j] = part[j].astype(jnp.bfloat16)

                    left(j).start()

        ke = s - last

        @pl.when((ke >= 0) & (ke < steps))
        def _():
            j = r * steps + ke

            @pl.when(r > 0)
            def _():
                right(j).wait_recv()
                part[j] = part[j] + r_buf[j].astype(jnp.float32)

            @pl.when(r < last)
            def _():
                left(j).wait_recv()
                part[j] = part[j] + l_buf[j].astype(jnp.float32)

            cot_copy(ke).wait()
            hidden = part[j]
            square = hidden * hidden
            tanh_val = jnp.tanh(root_two_pi * (hidden + cubic * square * hidden))
            half = 0.5 * (1.0 + tanh_val)
            act_buf[ke] = (hidden * half).astype(jnp.bfloat16)
            slope = half + 0.5 * hidden * (1.0 - tanh_val * tanh_val) * root_two_pi * (
                1.0 + 3.0 * cubic * square
            )
            g_buf[j] = (cot_buf[ke].astype(jnp.float32) * slope).astype(jnp.bfloat16)

            @pl.when(r < last)
            def _():
                g_right(j).start()

            @pl.when(r > 0)
            def _():
                g_left(j).start()

            act_copy(ke).start()
            share(r, ke)

        for away in range(1, rows):
            kg = s - last - away

            @pl.when((kg >= 0) & (kg < steps) & (r - away >= 0))
            def _():
                q = r - away
                j = q * steps + kg
                g_right(j).wait_recv()

                @pl.when(r < last)
                def _():
                    g_right(j).start()

                share(q, kg)

            @pl.when((kg >= 0) & (kg < steps) & (r + away <= last))
            def _():
                q = r + away
                j = q * steps + kg
                g_left(j).wait_recv()

                @pl.when(r > 0)
                def _():
                    g_left(j).start()

                share(q, kg)

        ki = s - 2 * last

        @pl.when((ki >= 0) & (ki < steps))
        def _():
            wide = 512 if features % 512 == 0 else features
            for n in range(0, features, wide):
                total = acc[:, n : n + wide]
                for q in range(rows):
                    j = q * steps + ki
                    total = total + lax.dot_general(
                        g_buf[j],
                        w_buf[j, n : n + wide, :],
                        (((1,), (1,)), ((), ())),
                        preferred_element_type=jnp.float32,
                    )
                acc[:, n : n + wide] = total

        return carry

    lax.fori_loop(0, steps + 2 * last, body, 0)

    half_rows = tokens // 2
    mine = lax.rem(c, 2)
    own_rows = pl.ds(pl.multiple_of(mine * half_rows, half_rows), half_rows)
    other_rows = pl.ds(pl.multiple_of((1 - mine) * half_rows, half_rows), half_rows)
    out_buf[0] = acc[other_rows, :].astype(jnp.bfloat16)
    swap = remote(out_buf.at[0], in_buf.at[0], cs_sem.at[0], cr_sem.at[0], {"col": twin})
    swap.start()
    swap.wait()
    out_buf[1] = (acc[own_rows, :] + in_buf[0].astype(jnp.float32)).astype(jnp.bfloat16)
    for bit in range(1, bits):
        swap = remote(
            out_buf.at[bit], in_buf.at[bit], cs_sem.at[bit], cr_sem.at[bit], {"col": flip(bit)}
        )
        swap.start()
        swap.wait()
        out_buf[bit + 1] = (
            out_buf[bit].astype(jnp.float32) + in_buf[bit].astype(jnp.float32)
        ).astype(jnp.bfloat16)
    result = out_buf.at[bits]
    final = remote(result, grad_out.at[own_rows, :], cs_sem.at[bits], cr_sem.at[bits], {"col": twin})
    keep = pltpu.make_async_copy(result, grad_out.at[own_rows, :], cs_sem.at[bits + 1])
    final.start()
    keep.start()

    for off in range(1, depths):
        target = lax.rem(d + off, depths)
        x_over(target).wait_send()
        source = lax.rem(d + depths - off, depths)
        remote(x_ref, x_place(source), in_sem.at[target], out_sem.at[source], {"depth": target}).wait_recv()
    x_keep.wait()

    def drain(k, carry):
        act_copy(k).wait()
        for q in range(rows):
            j = q * steps + k

            @pl.when(q > r)
            def _():
                right(j).wait_send()

            @pl.when(q < r)
            def _():
                left(j).wait_send()

            @pl.when((q <= r) & (r < last))
            def _():
                g_right(j).wait_send()

            @pl.when((q >= r) & (r > 0))
            def _():
                g_left(j).wait_send()

            @pl.when(q // per != d)
            def _():
                g_over(q, k).wait_send()

            @pl.when(q // per == d)
            def _():
                g_keep(q, k).wait()

        for off in range(1, depths):
            source = lax.rem(d + off, depths)
            for p in range(per):
                slot = (source * per + p) * steps + k
                remote(
                    g_buf.at[k], g_place(source, p, k), xs_sem.at[k], xr_sem.at[slot], {"depth": source}
                ).wait_recv()
        return carry

    lax.fori_loop(0, steps, drain, 0)
    keep.wait()
    final.wait_send()
    remote(
        result, grad_out.at[other_rows, :], cs_sem.at[bits], cr_sem.at[bits], {"col": twin}
    ).wait_recv()


def local(rows, depths, cols, inputs, weight, cotangent):
    tokens, features = inputs.shape
    units = weight.shape[1]
    width = units // rows
    chunk = 256 if width % 256 == 0 else width
    steps = width // chunk
    blocks = rows * steps
    bits = cols.bit_length() - 1
    bf16, f32 = jnp.bfloat16, jnp.float32
    dma = lambda n: pltpu.SemaphoreType.DMA((n,))
    anywhere = pl.BlockSpec(memory_space=pl.ANY)
    activated, input_grad, x_all, g_all = pl.pallas_call(
        functools.partial(kernel, rows, depths, cols),
        out_shape=(
            jax.ShapeDtypeStruct((tokens, width), bf16),
            jax.ShapeDtypeStruct((tokens, features), bf16),
            jax.ShapeDtypeStruct((depths * tokens, features), bf16),
            jax.ShapeDtypeStruct((depths * tokens, units // depths), bf16),
        ),
        in_specs=[pl.BlockSpec(memory_space=pltpu.VMEM), anywhere, anywhere],
        out_specs=(anywhere,) * 4,
        scratch_shapes=[
            pltpu.VMEM((blocks, features, chunk), bf16),
            pltpu.VMEM((blocks, tokens, chunk), f32),
            pltpu.VMEM((blocks, tokens, chunk), bf16),
            pltpu.VMEM((blocks, tokens, chunk), bf16),
            pltpu.VMEM((blocks, tokens, chunk), bf16),
            pltpu.VMEM((blocks, tokens, chunk), bf16),
            pltpu.VMEM((steps, tokens, chunk), bf16),
            pltpu.VMEM((steps, tokens, chunk), bf16),
            pltpu.VMEM((tokens, features), f32),
            pltpu.VMEM((bits + 1, tokens // 2, features), bf16),
            pltpu.VMEM((bits, tokens // 2, features), bf16),
            dma(blocks), dma(steps), dma(steps), dma(blocks), dma(blocks), dma(blocks),
            dma(blocks), dma(blocks), dma(blocks), dma(blocks), dma(depths * (rows // depths) * steps),
            dma(depths), dma(depths), dma(bits + 2), dma(bits + 1),
        ],
        compiler_params=pltpu.CompilerParams(
            collective_id=0, has_side_effects=True, vmem_limit_bytes=60 * 1024 * 1024
        ),
    )(inputs, weight, cotangent[:, 0, :])
    weight_grad = lax.dot_general(
        x_all, g_all, (((0,), (0,)), ((), ())), preferred_element_type=f32
    ).astype(bf16)
    return activated[:, None, :], input_grad, weight_grad[:, None, :]


def solution(mesh):
    shape = mesh.shape
    placed = (P("depth", "row"), P("row", "col"), P("depth", "col", "row"))
    return jax.shard_map(
        functools.partial(local, shape["row"], shape["depth"], shape["col"]),
        mesh=mesh,
        in_specs=placed,
        out_specs=(P("depth", "col", "row"), P("depth", "row"), P("row", "col", "depth")),
        check_vma=False,
    )
```

time: 662 us -> 131 us (0.20)
  waiting for transfers between devices: 544 us -> 0 us
  Pallas kernels: 0 us -> 119 us
  blocking collectives: 33.4 us -> 0 us
  matrix products: 39.2 us -> 9.51 us
  other arithmetic: 14.7 us -> 0 us
  local copies, waits for them, and re-layouts: 16.2 us -> 1.77 us
  between operations: 13.8 us -> 0.66 us
    reduce_scatter x2 -> x0, waiting for transfers between devices: 480 us -> none  [the longest x1 367 us: local(): lax.psum_scatter(weight_term[:, None, :], 'depth', scatter_dimension=2, t...]
    pallas_call x0 -> x1, Pallas kernels: none -> 119 us  [local(): pl.pallas_call(functools.partial(kernel, rows, depths, cols), out_shape=(...]
    all_gather x1 -> x0, waiting for transfers between devices: 64.1 us -> none  [local(): grad_hidden = lax.all_gather(grad_own, 'row', axis=1, tiled=True)]
    psum x1 -> x0, blocking collectives: 33.4 us -> none  [local(): input_grad = lax.psum(input_term, 'col').astype(jnp.bfloat16)]
    dot_general x3 -> x1, matrix products: 39.2 us -> 9.51 us  [local(): lax.dot_general(x_all, g_all, (((0,), (0,)), ((), ())), preferred_element...]
    convert_element_type x2 -> x0, other arithmetic: 14.7 us -> none  [the longest x1 11.3 us: local(): weight_grad = lax.psum_scatter(weight_term[:, None, :], 'depth', scatter_...]
    unnamed x9 -> x6, local copies, waits for them, and re-layouts: 16.2 us -> 1.77 us
  transfers between devices with their start and end apart: 3 -> 0, of which waited for: 3 -> 0; matrix products, arithmetic and copies ran while one was open for 2% -> 0% of each run, Pallas kernels for 0% -> 0%
where the time goes in v1:
time: 131 us
  Pallas kernels  119 us (91%)
  matrix products  9.51 us (7%)
  local copies, waits for them, and re-layouts  1.77 us (1%)
    pallas_call x1, Pallas kernels, local(): pl.pallas_call(functools.partial(kernel, rows, depths, cols), out_shape=(...  119 us
    dot_general x1, matrix products, local(): lax.dot_general(x_all, g_all, (((0,), (0,)), ((), ())), preferred_element...  9.51 us

profile of v1, /device:TPU:0, one launch (start us, length us, event | category | flops | bytes accessed | tf_op | source)
XLA Modules:
  0.0 131.0 jit_solution(6538118168471433518)
XLA Ops:
  0.6 119.0 %shard_map.58 = (bf16[256,1536]{1,0:T(8,128)(2,1)}, bf16[256,1536]{1,0:T(8,128)(2,1)}, bf16[512,1536]{1,0:T(8,128)(2,1)}, bf16[512,3072]{1,0:T(8,128)(2,1)}) custom-call(bf16[256,1536]{1,0:T(8,128)(2,1)} %x_ref.1, bf16[1536,6144]{1,0:T(8,128)(2,1)} %w_hbm.1, bf16[256,1536]{1,0:T(8,128)(2,1)} %bitcast.6), custom_call_target="tpu_custom_call" | custom-call | tf_op jit(solution)/shard_map/pallas_call | solution.py:364
  119.7 0.0 copy-start.1
  119.7 0.0 copy-start
  119.7 9.5 %fusion = bf16[1536,1,3072]{2,0,1:T(8,128)(2,1)} fusion(bf16[512,1536]{1,0:T(8,128)(2,1)} %get-tuple-element.9, bf16[512,3072]{1,0:T(8,128)(2,1)} %get-tuple-element.10), kind=kOutput, calls=%fused_computation.1 | convolution fusion | flops 4836556800 | bytes 14155776 | tf_op jit(solution)/shard_map/dot_general | solution.py:394
  129.2 0.0 copy-done.1
  129.2 0.9 copy.8
  130.1 0.0 copy-done
  130.1 0.9 copy.9
Async XLA Ops:
  119.7 9.5 %copy-start.1 = (bf16[256,1536]{1,0:T(8,128)(2,1)S(1)}, bf16[256,1536]{1,0:T(8,128)(2,1)}, u32[]{:S(2)}) copy-start(bf16[256,1536]{1,0:T(8,128)(2,1)} %get-tuple-element.7) | copy-start | bytes 2359300
  119.7 10.4 %copy-start = (bf16[256,1536]{1,0:T(8,128)(2,1)S(1)}, bf16[256,1536]{1,0:T(8,128)(2,1)}, u32[]{:S(2)}) copy-start(bf16[256,1536]{1,0:T(8,128)(2,1)} %get-tuple-element.15) | copy-start | bytes 2359300

commit v2 on v1

--- a/solution.py
+++ b/solution.py
@@ -24,7 +24,7 @@
 
 
 def kernel(
-    rows, depths, cols, x_ref, w_hbm, cot_hbm,
+    rows, depths, cols, groups, x_ref, w_hbm, cot_hbm,
     act_out, grad_out, x_all, g_all,
     w_buf, part, s_buf, r_buf, l_buf, g_buf, cot_buf, act_buf, acc, out_buf, in_buf,
     w_sem, cot_sem, act_sem, s_sem, r_sem, l_sem, g_sem, gr_sem, gl_sem, xs_sem, xr_sem,
@@ -33,8 +33,10 @@
     r, d, c = lax.axis_index("row"), lax.axis_index("depth"), lax.axis_index("col")
     tokens, features = x_ref.shape
     chunk = w_buf.shape[2]
-    steps = w_buf.shape[0] // rows
-    width = steps * chunk
+    parts = w_buf.shape[0] // rows
+    steps = parts * groups
+    width = parts * chunk
+    span = tokens // groups
     per = rows // depths
     last = rows - 1
     twin = c + 1 - 2 * lax.rem(c, 2)
@@ -45,17 +47,25 @@
         return c + size - 2 * size * lax.rem(c // size, 2)
 
     def w_copy(q, k):
-        j = q * steps + k
+        j = q * parts + k
         at = pl.multiple_of(q * width + k * chunk, chunk)
         return pltpu.make_async_copy(w_hbm.at[:, pl.ds(at, chunk)], w_buf.at[j], w_sem.at[j])
 
+    def rows_of(k, base):
+        return pl.ds(pl.multiple_of(base + lax.div(k, parts) * span, span), span)
+
+    def cols_of(k, base):
+        return pl.ds(pl.multiple_of(base + lax.rem(k, parts) * chunk, chunk), chunk)
+
     def cot_copy(k):
-        at = pl.multiple_of(k * chunk, chunk)
-        return pltpu.make_async_copy(cot_hbm.at[:, pl.ds(at, chunk)], cot_buf.at[k], cot_sem.at[k])
+        return pltpu.make_async_copy(
+            cot_hbm.at[rows_of(k, 0), cols_of(k, 0)], cot_buf.at[k], cot_sem.at[k]
+        )
 
     def act_copy(k):
-        at = pl.multiple_of(k * chunk, chunk)
-        return pltpu.make_async_copy(act_buf.at[k], act_out.at[:, pl.ds(at, chunk)], act_sem.at[k])
+        return pltpu.make_async_copy(
+            act_buf.at[k], act_out.at[rows_of(k, 0), cols_of(k, 0)], act_sem.at[k]
+        )
 
     def right(j):
         return remote(s_buf.at[j], r_buf.at[j], s_sem.at[j], r_sem.at[j], {"row": r + 1})
@@ -70,8 +80,7 @@
         return remote(g_buf.at[j], g_buf.at[j], gl_sem.at[j], g_sem.at[j], {"row": r - 1})
 
     def g_place(source, q, k):
-        at = pl.multiple_of(lax.rem(q, per) * width + k * chunk, chunk)
-        return g_all.at[pl.ds(pl.multiple_of(source * tokens, tokens), tokens), pl.ds(at, chunk)]
+        return g_all.at[rows_of(k, source * tokens), cols_of(k, lax.rem(q, per) * width)]
 
     def g_over(q, k):
         j = q * steps + k
@@ -103,10 +112,15 @@
 
     x_keep = pltpu.make_async_copy(x_ref, x_place(d), in_sem.at[d])
 
-    for k in range(steps):
+    for k in range(parts):
         for q in range(rows):
             w_copy(q, k).start()
+
+    def fetch(k, carry):
         cot_copy(k).start()
+        return carry
+
+    lax.fori_loop(0, steps, fetch, 0)
     x_keep.start()
 
     barrier = pltpu.get_barrier_semaphore()
@@ -139,14 +153,53 @@
 
     acc[...] = jnp.zeros_like(acc)
 
+    def project(k):
+        if isinstance(k, int):
+            k = jnp.int32(k)
+        p = lax.rem(k, parts)
+
+        @pl.when(k < parts)
+        def _():
+            for q in range(rows):
+                w_copy(q, p).wait()
+
+        for q in range(rows):
+            part[q * steps + k] = jnp.dot(
+                x_ref[rows_of(k, 0), :], w_buf[q * parts + p], preferred_element_type=jnp.float32
+            )
+
+    def lag(q):
+        return jnp.maximum(q, last - q)
+
+    half = span // 2
+    mine = lax.rem(c, 2)
+
+    def half_at(t, which):
+        return pl.ds(pl.multiple_of(t * span + which * half, half), half)
+
+    def swap(t, bit):
+        return remote(
+            out_buf.at[bit, t], in_buf.at[bit, t], cs_sem.at[bit, t], cr_sem.at[bit, t],
+            {"col": flip(bit)},
+        )
+
+    def final(t, which):
+        return remote(
+            out_buf.at[bits, t], grad_out.at[half_at(t, which), :], cs_sem.at[bits, t],
+            cr_sem.at[bits, t], {"col": twin},
+        )
+
+    def keep(t):
+        return pltpu.make_async_copy(
+            out_buf.at[bits, t], grad_out.at[half_at(t, mine), :], cs_sem.at[bits + 1, t]
+        )
+
+    def ended(k):
+        return (k >= 0) & (k < steps) & (lax.rem(k, parts) == parts - 1)
+
+    project(0)
+
     def body(s, carry):
-        @pl.when(s < steps)
-        def _():
-            for q in range(rows):
-                j = q * steps + s
-                w_copy(q, s).wait()
-                part[j] = jnp.dot(x_ref[...], w_buf[j], preferred_element_type=jnp.float32)
-
         kr = s - r
 
         @pl.when((kr >= 0) & (kr < steps))
@@ -187,7 +240,7 @@
 
                     left(j).start()
 
-        ke = s - last
+        ke = s - lag(r)
 
         @pl.when((ke >= 0) & (ke < steps))
         def _():
@@ -207,9 +260,9 @@
             hidden = part[j]
             square = hidden * hidden
             tanh_val = jnp.tanh(root_two_pi * (hidden + cubic * square * hidden))
-            half = 0.5 * (1.0 + tanh_val)
-            act_buf[ke] = (hidden * half).astype(jnp.bfloat16)
-            slope = half + 0.5 * hidden * (1.0 - tanh_val * tanh_val) * root_two_pi * (
+            gate = 0.5 * (1.0 + tanh_val)
+            act_buf[ke] = (hidden * gate).astype(jnp.bfloat16)
+            slope = gate + 0.5 * hidden * (1.0 - tanh_val * tanh_val) * root_two_pi * (
                 1.0 + 3.0 * cubic * square
             )
             g_buf[j] = (cot_buf[ke].astype(jnp.float32) * slope).astype(jnp.bfloat16)
@@ -226,76 +279,79 @@
             share(r, ke)
 
         for away in range(1, rows):
-            kg = s - last - away
-
-            @pl.when((kg >= 0) & (kg < steps) & (r - away >= 0))
+            ka = s - lag(r - away) - away
+
+            @pl.when((ka >= 0) & (ka < steps) & (r - away >= 0))
             def _():
                 q = r - away
-                j = q * steps + kg
+                j = q * steps + ka
                 g_right(j).wait_recv()
 
                 @pl.when(r < last)
                 def _():
                     g_right(j).start()
 
-                share(q, kg)
-
-            @pl.when((kg >= 0) & (kg < steps) & (r + away <= last))
+                share(q, ka)
+
+            kb = s - lag(r + away) - away
+
+            @pl.when((kb >= 0) & (kb < steps) & (r + away <= last))
             def _():
                 q = r + away
-                j = q * steps + kg
+                j = q * steps + kb
                 g_left(j).wait_recv()
 
                 @pl.when(r > 0)
                 def _():
                     g_left(j).start()
 
-                share(q, kg)
+                share(q, kb)
+
+        @pl.when(s + 1 < steps)
+        def _():
+            project(s + 1)
 
         ki = s - 2 * last
 
         @pl.when((ki >= 0) & (ki < steps))
         def _():
+            p = lax.rem(ki, parts)
             wide = 512 if features % 512 == 0 else features
             for n in range(0, features, wide):
-                total = acc[:, n : n + wide]
+                total = acc[rows_of(ki, 0), n : n + wide]
                 for q in range(rows):
-                    j = q * steps + ki
                     total = total + lax.dot_general(
-                        g_buf[j],
-                        w_buf[j, n : n + wide, :],
+                        g_buf[q * steps + ki],
+                        w_buf[q * parts + p, n : n + wide, :],
                         (((1,), (1,)), ((), ())),
                         preferred_element_type=jnp.float32,
                     )
-                acc[:, n : n + wide] = total
+                acc[rows_of(ki, 0), n : n + wide] = total
+
+        @pl.when(ended(ki))
+        def _():
+            t = lax.div(ki, parts)
+            out_buf[0, t] = acc[half_at(t, 1 - mine), :].astype(jnp.bfloat16)
+            swap(t, 0).start()
+
+        for bit in range(bits):
+            kc = ki - 1 - 2 * bit
+
+            @pl.when(ended(kc))
+            def _():
+                t = lax.div(kc, parts)
+                swap(t, bit).wait_recv()
+                own = acc[half_at(t, mine), :] if bit == 0 else out_buf[bit, t].astype(jnp.float32)
+                out_buf[bit + 1, t] = (own + in_buf[bit, t].astype(jnp.float32)).astype(jnp.bfloat16)
+                if bit + 1 < bits:
+                    swap(t, bit + 1).start()
+                else:
+                    final(t, mine).start()
+                    keep(t).start()
 
         return carry
 
-    lax.fori_loop(0, steps + 2 * last, body, 0)
-
-    half_rows = tokens // 2
-    mine = lax.rem(c, 2)
-    own_rows = pl.ds(pl.multiple_of(mine * half_rows, half_rows), half_rows)
-    other_rows = pl.ds(pl.multiple_of((1 - mine) * half_rows, half_rows), half_rows)
-    out_buf[0] = acc[other_rows, :].astype(jnp.bfloat16)
-    swap = remote(out_buf.at[0], in_buf.at[0], cs_sem.at[0], cr_sem.at[0], {"col": twin})
-    swap.start()
-    swap.wait()
-    out_buf[1] = (acc[own_rows, :] + in_buf[0].astype(jnp.float32)).astype(jnp.bfloat16)
-    for bit in range(1, bits):
-        swap = remote(
-            out_buf.at[bit], in_buf.at[bit], cs_sem.at[bit], cr_sem.at[bit], {"col": flip(bit)}
-        )
-        swap.start()
-        swap.wait()
-        out_buf[bit + 1] = (
-            out_buf[bit].astype(jnp.float32) + in_buf[bit].astype(jnp.float32)
-        ).astype(jnp.bfloat16)
-    result = out_buf.at[bits]
-    final = remote(result, grad_out.at[own_rows, :], cs_sem.at[bits], cr_sem.at[bits], {"col": twin})
-    keep = pltpu.make_async_copy(result, grad_out.at[own_rows, :], cs_sem.at[bits + 1])
-    final.start()
-    keep.start()
+    lax.fori_loop(0, steps + 2 * last + 2 * bits - 1, body, 0)
 
     for off in range(1, depths):
         target = lax.rem(d + off, depths)
@@ -343,26 +399,30 @@
         return carry
 
     lax.fori_loop(0, steps, drain, 0)
-    keep.wait()
-    final.wait_send()
-    remote(
-        result, grad_out.at[other_rows, :], cs_sem.at[bits], cr_sem.at[bits], {"col": twin}
-    ).wait_recv()
+    for t in range(groups):
+        for bit in range(bits):
+            swap(t, bit).wait_send()
+        keep(t).wait()
+        final(t, mine).wait_send()
+        final(t, 1 - mine).wait_recv()
 
 
 def local(rows, depths, cols, inputs, weight, cotangent):
     tokens, features = inputs.shape
     units = weight.shape[1]
     width = units // rows
+    groups = 2
     chunk = 256 if width % 256 == 0 else width
-    steps = width // chunk
+    parts = width // chunk
+    steps = parts * groups
+    span = tokens // groups
     blocks = rows * steps
     bits = cols.bit_length() - 1
     bf16, f32 = jnp.bfloat16, jnp.float32
-    dma = lambda n: pltpu.SemaphoreType.DMA((n,))
+    dma = lambda *n: pltpu.SemaphoreType.DMA(n)
     anywhere = pl.BlockSpec(memory_space=pl.ANY)
     activated, input_grad, x_all, g_all = pl.pallas_call(
-        functools.partial(kernel, rows, depths, cols),
+        functools.partial(kernel, rows, depths, cols, groups),
         out_shape=(
             jax.ShapeDtypeStruct((tokens, width), bf16),
             jax.ShapeDtypeStruct((tokens, features), bf16),
@@ -372,20 +432,20 @@
         in_specs=[pl.BlockSpec(memory_space=pltpu.VMEM), anywhere, anywhere],
         out_specs=(anywhere,) * 4,
         scratch_shapes=[
-            pltpu.VMEM((blocks, features, chunk), bf16),
-            pltpu.VMEM((blocks, tokens, chunk), f32),
-            pltpu.VMEM((blocks, tokens, chunk), bf16),
-            pltpu.VMEM((blocks, tokens, chunk), bf16),
-            pltpu.VMEM((blocks, tokens, chunk), bf16),
-            pltpu.VMEM((blocks, tokens, chunk), bf16),
-            pltpu.VMEM((steps, tokens, chunk), bf16),
-            pltpu.VMEM((steps, tokens, chunk), bf16),
+            pltpu.VMEM((rows * parts, features, chunk), bf16),
+            pltpu.VMEM((blocks, span, chunk), f32),
+            pltpu.VMEM((blocks, span, chunk), bf16),
+            pltpu.VMEM((blocks, span, chunk), bf16),
+            pltpu.VMEM((blocks, span, chunk), bf16),
+            pltpu.VMEM((blocks, span, chunk), bf16),
+            pltpu.VMEM((steps, span, chunk), bf16),
+            pltpu.VMEM((steps, span, chunk), bf16),
             pltpu.VMEM((tokens, features), f32),
-            pltpu.VMEM((bits + 1, tokens // 2, features), bf16),
-            pltpu.VMEM((bits, tokens // 2, features), bf16),
-            dma(blocks), dma(steps), dma(steps), dma(blocks), dma(blocks), dma(blocks),
+            pltpu.VMEM((bits + 1, groups, span // 2, features), bf16),
+            pltpu.VMEM((bits, groups, span // 2, features), bf16),
+            dma(rows * parts), dma(steps), dma(steps), dma(blocks), dma(blocks), dma(blocks),
             dma(blocks), dma(blocks), dma(blocks), dma(blocks), dma(depths * (rows // depths) * steps),
-            dma(depths), dma(depths), dma(bits + 2), dma(bits + 1),
+            dma(depths), dma(depths), dma(bits + 2, groups), dma(bits + 1, groups),
         ],
         compiler_params=pltpu.CompilerParams(
             collective_id=0, has_side_effects=True, vmem_limit_bytes=60 * 1024 * 1024

time: 131 us -> 114 us (0.87)
  Pallas kernels: 119 us -> 102 us
    pallas_call x1, Pallas kernels: 119 us -> 102 us  [local(): pl.pallas_call(functools.partial(kernel, rows, depths, cols, groups), out...]
where the time goes in v2:
time: 114 us
  Pallas kernels  102 us (89%)
  matrix products  9.51 us (8%)
  local copies, waits for them, and re-layouts  1.77 us (2%)
    pallas_call x1, Pallas kernels, local(): pl.pallas_call(functools.partial(kernel, rows, depths, cols, groups), out...  102 us
    dot_general x1, matrix products, local(): lax.dot_general(x_all, g_all, (((0,), (0,)), ((), ())), preferred_element...  9.51 us

profile of v2, /device:TPU:0, one launch (start us, length us, event | category | flops | bytes accessed | tf_op | source)
XLA Modules:
  0.0 113.6 jit_solution(13377242535536006060)
XLA Ops:
  0.6 101.7 %shard_map.58 = (bf16[256,1536]{1,0:T(8,128)(2,1)}, bf16[256,1536]{1,0:T(8,128)(2,1)}, bf16[512,1536]{1,0:T(8,128)(2,1)}, bf16[512,3072]{1,0:T(8,128)(2,1)}) custom-call(bf16[256,1536]{1,0:T(8,128)(2,1)} %x_ref.1, bf16[1536,6144]{1,0:T(8,128)(2,1)} %w_hbm.1, bf16[256,1536]{1,0:T(8,128)(2,1)} %bitcast.6), custom_call_target="tpu_custom_call" | custom-call | tf_op jit(solution)/shard_map/pallas_call | solution.py:424
  102.3 0.0 copy-start.1
  102.4 0.0 copy-start
  102.4 9.5 %fusion = bf16[1536,1,3072]{2,0,1:T(8,128)(2,1)} fusion(bf16[512,1536]{1,0:T(8,128)(2,1)} %get-tuple-element.9, bf16[512,3072]{1,0:T(8,128)(2,1)} %get-tuple-element.10), kind=kOutput, calls=%fused_computation.1 | convolution fusion | flops 4836556800 | bytes 14155776 | tf_op jit(solution)/shard_map/dot_general | solution.py:454
  111.9 0.0 copy-done.1
  111.9 0.9 copy.8
  112.8 0.0 copy-done
  112.8 0.9 copy.9
Async XLA Ops:
  102.3 9.5 %copy-start.1 = (bf16[256,1536]{1,0:T(8,128)(2,1)S(1)}, bf16[256,1536]{1,0:T(8,128)(2,1)}, u32[]{:S(2)}) copy-start(bf16[256,1536]{1,0:T(8,128)(2,1)} %get-tuple-element.7) | copy-start | bytes 2359300
  102.4 10.4 %copy-start = (bf16[256,1536]{1,0:T(8,128)(2,1)S(1)}, bf16[256,1536]{1,0:T(8,128)(2,1)}, u32[]{:S(2)}) copy-start(bf16[256,1536]{1,0:T(8,128)(2,1)} %get-tuple-element.15) | copy-start | bytes 2359300

commit v3 on v2

--- a/solution.py
+++ b/solution.py
@@ -112,7 +112,7 @@
 
     x_keep = pltpu.make_async_copy(x_ref, x_place(d), in_sem.at[d])
 
-    for k in range(parts):
+    for k in range(min(2, parts)):
         for q in range(rows):
             w_copy(q, k).start()
 
@@ -162,6 +162,11 @@
         def _():
             for q in range(rows):
                 w_copy(q, p).wait()
+
+        @pl.when(k + 2 < parts)
+        def _():
+            for q in range(rows):
+                w_copy(q, p + 2).start()
 
         for q in range(rows):
             part[q * steps + k] = jnp.dot(

time: 114 us -> 114 us (level)
  no operation moved by 1% of the time
where the time goes in v3:
time: 114 us
  Pallas kernels  102 us (89%)
  matrix products  9.51 us (8%)
  local copies, waits for them, and re-layouts  1.77 us (2%)
    pallas_call x1, Pallas kernels, local(): pl.pallas_call(functools.partial(kernel, rows, depths, cols, groups), out...  102 us
    dot_general x1, matrix products, local(): lax.dot_general(x_all, g_all, (((0,), (0,)), ((), ())), preferred_element...  9.51 us

profile of v3, /device:TPU:0, one launch (start us, length us, event | category | flops | bytes accessed | tf_op | source)
XLA Modules:
  0.0 113.6 jit_solution(651825323282097960)
XLA Ops:
  0.6 101.7 %shard_map.58 = (bf16[256,1536]{1,0:T(8,128)(2,1)}, bf16[256,1536]{1,0:T(8,128)(2,1)}, bf16[512,1536]{1,0:T(8,128)(2,1)}, bf16[512,3072]{1,0:T(8,128)(2,1)}) custom-call(bf16[256,1536]{1,0:T(8,128)(2,1)} %x_ref.1, bf16[1536,6144]{1,0:T(8,128)(2,1)} %w_hbm.1, bf16[256,1536]{1,0:T(8,128)(2,1)} %bitcast.6), custom_call_target="tpu_custom_call" | custom-call | tf_op jit(solution)/shard_map/pallas_call | solution.py:429
  102.3 0.0 copy-start.1
  102.4 0.0 copy-start
  102.4 9.5 %fusion = bf16[1536,1,3072]{2,0,1:T(8,128)(2,1)} fusion(bf16[512,1536]{1,0:T(8,128)(2,1)} %get-tuple-element.9, bf16[512,3072]{1,0:T(8,128)(2,1)} %get-tuple-element.10), kind=kOutput, calls=%fused_computation.1 | convolution fusion | flops 4836556800 | bytes 14155776 | tf_op jit(solution)/shard_map/dot_general | solution.py:459
  111.9 0.0 copy-done.1
  111.9 0.9 copy.8
  112.8 0.0 copy-done
  112.8 0.9 copy.9
Async XLA Ops:
  102.3 9.5 %copy-start.1 = (bf16[256,1536]{1,0:T(8,128)(2,1)S(1)}, bf16[256,1536]{1,0:T(8,128)(2,1)}, u32[]{:S(2)}) copy-start(bf16[256,1536]{1,0:T(8,128)(2,1)} %get-tuple-element.7) | copy-start | bytes 2359300
  102.4 10.4 %copy-start = (bf16[256,1536]{1,0:T(8,128)(2,1)S(1)}, bf16[256,1536]{1,0:T(8,128)(2,1)}, u32[]{:S(2)}) copy-start(bf16[256,1536]{1,0:T(8,128)(2,1)} %get-tuple-element.15) | copy-start | bytes 2359300
